TPU v7x, 32 devices: a whole 2x2x4 slice. The times are simulated.
32 devices in a mesh: grp: 8 (over z, y), seq: 4 (over x, core).
Axes of the slice: x: 2, y: 2, z: 4, core: 2. Of those that a mesh axis runs over, the one named last changes fastest.
Arguments:
- tokens_in: bfloat16 [24576, 768], P(('grp', 'seq')), may hold values from -6 to 6
- lengths: int32 [8], P('grp'), may hold values from 2305 to 3072, as said below
- ln1_gain: float32 [768], replicated, may hold values from 0.5 to 1.5
- ln1_bias: float32 [768], replicated, may hold values from -1.75 to 1.75
- w_qkv: bfloat16 [768, 2304], replicated, may hold values from -0.21875 to 0.21875
- bias_query: float32 [768], replicated, may hold values from -1.75 to 1.75
- bias_value: float32 [768], replicated, may hold values from -1.75 to 1.75
- w_out: bfloat16 [768, 768], replicated, may hold values from -0.875 to 0.875
- bias_out: float32 [768], replicated, may hold values from -1.75 to 1.75
- ln2_gain: float32 [768], replicated, may hold values from 0.5 to 1.5
- ln2_bias: float32 [768], replicated, may hold values from -1.75 to 1.75
- w_up: bfloat16 [768, 3072], replicated, may hold values from -0.21875 to 0.21875
- bias_up: float32 [3072], replicated, may hold values from -1.75 to 1.75
- w_down: bfloat16 [3072, 768], replicated, may hold values from -0.109375 to 0.109375
- bias_down: float32 [768], replicated, may hold values from -1.75 to 1.75
- proj_patch: bfloat16 [768, 768], replicated, may hold values from -0.21875 to 0.21875
- proj_class: bfloat16 [768, 768], replicated, may hold values from -0.21875 to 0.21875
- class_emb: bfloat16 [150, 768], replicated, may hold values from -6 to 6
- d_masks: bfloat16 [24576, 150], P(('grp', 'seq')), may hold values from -6 to 6
Outputs:
- masks: bfloat16 [24576, 150], P(('grp', 'seq'))
- grad_tokens: bfloat16 [24576, 768], P(('grp', 'seq'))
- grad_ln1_gain: float32 [768], P('grp')
- grad_ln1_bias: float32 [768], P('grp')
- grad_w_qkv: float32 [768, 2304], P('grp', 'seq')
- grad_bias_query: float32 [768], P('grp')
- grad_bias_value: float32 [768], P('grp')
- grad_w_out: float32 [768, 768], P('grp', 'seq')
- grad_bias_out: float32 [768], P('grp')
- grad_ln2_gain: float32 [768], P('grp')
- grad_ln2_bias: float32 [768], P('grp')
- grad_w_up: float32 [768, 3072], P('grp', 'seq')
- grad_bias_up: float32 [3072], P('grp')
- grad_w_down: float32 [3072, 768], P('grp', 'seq')
- grad_bias_down: float32 [768], P('grp')
- grad_proj_patch: float32 [768, 768], P('grp', 'seq')
- grad_proj_class: float32 [768, 768], P('grp', 'seq')
- grad_class_emb: float32 [150, 768], P(None, 'grp')
Inputs may be any that keep to these rules, and one draw needn't show every extreme that they name: Image g fills the first lengths[g] rows of its 3072 rows, the rest is padding; in every draw some image has exactly 3072 rows.
All inputs are finite; a program needn't handle non-finite values.
Results may differ from a plain program's by a relative error of at most 0.015.
Values may be sent and summed in bfloat16 or wider, within the bound.
A program may use at most 256 MiB of HBM per device.

v0:
```python
import math
import jax
import jax.numpy as jnp
from jax import lax
from jax.sharding import PartitionSpec as P

HEAD_DIM = 64
EPS_NORM = 1e-06
EPS_UNIT = 1e-06
NEG_FILL = -1e30


def layer_norm(matrix_rows, gain_vec, shift_vec):
    row_mean = jnp.mean(matrix_rows, axis=-1, keepdims=True)
    centred = matrix_rows - row_mean
    row_var = jnp.mean(centred * centred, axis=-1, keepdims=True)
    return centred * lax.rsqrt(row_var + EPS_NORM) * gain_vec + shift_vec


def unit_rows(matrix_rows):
    return matrix_rows * lax.rsqrt(
        jnp.sum(matrix_rows * matrix_rows, axis=-1, keepdims=True) + EPS_UNIT
    )


def gelu_exact(values_in):
    return jax.nn.gelu(values_in, approximate=False)


def score_block(query_heads, key_block, keep_block, score_scale):
    scores = (
        jnp.einsum("qhd,khd->hqk", query_heads, key_block, preferred_element_type=jnp.float32)
        * score_scale
    )
    return jnp.where(keep_block[None, None, :], scores, NEG_FILL)


def split_blocks(key_heads, value_heads, key_keep, key_span):
    block_count = key_heads.shape[0] // key_span
    head_count = key_heads.shape[1]
    key_blocks = key_heads.reshape(block_count, key_span, head_count, -1)
    value_blocks = value_heads.reshape(block_count, key_span, head_count, -1)
    keep_blocks = key_keep.reshape(block_count, key_span)
    return (key_blocks, value_blocks, keep_blocks)


def attend_forward(query_heads, key_heads, value_heads, key_keep, score_scale, key_span):
    row_count, head_count = (query_heads.shape[0], query_heads.shape[1])
    key_blocks, value_blocks, keep_blocks = split_blocks(key_heads, value_heads, key_keep, key_span)

    def gather_stats(carried, pieces):
        row_top, row_total = carried
        key_block, keep_block = pieces
        scores = score_block(query_heads, key_block, keep_block, score_scale)
        new_top = jnp.maximum(row_top, jnp.max(scores, axis=-1))
        row_total = row_total * jnp.exp(row_top - new_top) + jnp.sum(
            jnp.exp(scores - new_top[..., None]), axis=-1
        )
        return ((new_top, row_total), None)

    start_stats = (
        jnp.full((head_count, row_count), NEG_FILL, jnp.float32),
        jnp.zeros((head_count, row_count), jnp.float32),
    )
    row_top, row_total = lax.scan(gather_stats, start_stats, (key_blocks, keep_blocks))[0]
    log_mass = row_top + jnp.log(row_total)

    def weigh_values(summed, pieces):
        key_block, value_block, keep_block = pieces
        scores = score_block(query_heads, key_block, keep_block, score_scale)
        prob_low = jnp.exp(scores - log_mass[..., None]).astype(jnp.bfloat16)
        summed = summed + jnp.einsum(
            "hqk,khd->qhd", prob_low, value_block, preferred_element_type=jnp.float32
        )
        return (summed, None)

    start_sum = jnp.zeros(query_heads.shape, jnp.float32)
    attended = lax.scan(weigh_values, start_sum, (key_blocks, value_blocks, keep_blocks))[0]
    return (attended, log_mass)


def attend_backward(
    query_heads,
    key_heads,
    value_heads,
    key_keep,
    grad_heads,
    log_mass,
    attended,
    score_scale,
    key_span,
):
    head_count = query_heads.shape[1]
    key_blocks, value_blocks, keep_blocks = split_blocks(key_heads, value_heads, key_keep, key_span)
    row_delta = jnp.einsum("qhd,qhd->hq", grad_heads.astype(jnp.float32), attended)

    def spread_grads(grad_query, pieces):
        key_block, value_block, keep_block = pieces
        prob_rows = jnp.exp(
            score_block(query_heads, key_block, keep_block, score_scale) - log_mass[..., None]
        )
        grad_probs = jnp.einsum(
            "qhd,khd->hqk", grad_heads, value_block, preferred_element_type=jnp.float32
        )
        grad_scores = (prob_rows * (grad_probs - row_delta[..., None])).astype(jnp.bfloat16)
        grad_query = grad_query + jnp.einsum(
            "hqk,khd->qhd", grad_scores, key_block, preferred_element_type=jnp.float32
        )
        grad_key_block = (
            jnp.einsum("hqk,qhd->khd", grad_scores, query_heads, preferred_element_type=jnp.float32)
            * score_scale
        )
        grad_value_block = jnp.einsum(
            "hqk,qhd->khd",
            prob_rows.astype(jnp.bfloat16),
            grad_heads,
            preferred_element_type=jnp.float32,
        )
        return (grad_query, (grad_key_block, grad_value_block))

    start_query = jnp.zeros(query_heads.shape, jnp.float32)
    grad_query, block_grads = lax.scan(
        spread_grads, start_query, (key_blocks, value_blocks, keep_blocks)
    )
    total_rows = key_heads.shape[0]
    model_width = head_count * query_heads.shape[2]
    grad_key_all = block_grads[0].reshape(total_rows, model_width)
    grad_value_all = block_grads[1].reshape(total_rows, model_width)
    return (grad_query * score_scale, grad_key_all, grad_value_all)


def column_sum(matrix_low):
    return jnp.sum(matrix_low.astype(jnp.float32), axis=0)


def body(
    tokens_in,
    lengths,
    ln1_gain,
    ln1_bias,
    w_qkv,
    bias_query,
    bias_value,
    w_out,
    bias_out,
    ln2_gain,
    ln2_bias,
    w_up,
    bias_up,
    w_down,
    bias_down,
    proj_patch,
    proj_class,
    class_emb,
    d_masks,
):
    row_count, model_width = tokens_in.shape
    head_size = HEAD_DIM
    head_count = model_width // head_size
    seq_devices = lax.axis_size("seq")
    grp_devices = lax.axis_size("grp")
    seq_total = row_count * seq_devices
    key_span = min(512, seq_total)
    score_scale = head_size ** (-0.5)
    mask_scale = math.sqrt(model_width)
    length_here = lengths[0]
    first_row = lax.axis_index("seq") * row_count
    valid_rows = (first_row + jnp.arange(row_count, dtype=jnp.int32) < length_here).astype(
        jnp.float32
    )
    key_keep = jnp.arange(seq_total, dtype=jnp.int32) < length_here
    tokens = tokens_in.astype(jnp.float32)
    normed_one, norm_one_back = jax.vjp(layer_norm, tokens, ln1_gain, ln1_bias)
    normed_low = normed_one.astype(jnp.bfloat16)
    zero_keys = jnp.zeros_like(bias_query)
    mixed = jnp.dot(normed_low, w_qkv, preferred_element_type=jnp.float32)
    mixed = mixed + jnp.concatenate([bias_query, zero_keys, bias_value])
    mixed_low = mixed.astype(jnp.bfloat16)
    query_heads = mixed_low[:, :model_width].reshape(row_count, head_count, head_size)
    key_rows = mixed_low[:, model_width : 2 * model_width]
    value_rows = mixed_low[:, 2 * model_width :]
    key_all, value_all = (
        lax.all_gather(key_rows, "seq", axis=0, tiled=True),
        lax.all_gather(value_rows, "seq", axis=0, tiled=True),
    )
    key_heads = key_all.reshape(seq_total, head_count, head_size)
    value_heads = value_all.reshape(seq_total, head_count, head_size)
    attended, log_mass = attend_forward(
        query_heads, key_heads, value_heads, key_keep, score_scale, key_span
    )
    attended_low = attended.reshape(row_count, model_width).astype(jnp.bfloat16)
    branch = jnp.dot(attended_low, w_out, preferred_element_type=jnp.float32) + bias_out
    middle = tokens + branch
    normed_two, norm_two_back = jax.vjp(layer_norm, middle, ln2_gain, ln2_bias)
    normed_two_low = normed_two.astype(jnp.bfloat16)
    hidden = jnp.dot(normed_two_low, w_up, preferred_element_type=jnp.float32) + bias_up
    active, gelu_back = jax.vjp(gelu_exact, hidden)
    active_low = active.astype(jnp.bfloat16)
    final = middle + (jnp.dot(active_low, w_down, preferred_element_type=jnp.float32) + bias_down)
    final_low = final.astype(jnp.bfloat16)
    patches = jnp.dot(final_low, proj_patch, preferred_element_type=jnp.float32)
    patch_unit, patch_back = jax.vjp(unit_rows, patches)
    patch_low = patch_unit.astype(jnp.bfloat16)
    classes = jnp.dot(class_emb, proj_class, preferred_element_type=jnp.float32)
    class_unit, class_back = jax.vjp(unit_rows, classes)
    class_low = class_unit.astype(jnp.bfloat16)
    mask_out = jnp.einsum("rd,cd->rc", patch_low, class_low, preferred_element_type=jnp.float32)
    mask_out = (mask_out * mask_scale * valid_rows[:, None]).astype(jnp.bfloat16)
    mask_grad = (d_masks.astype(jnp.float32) * valid_rows[:, None]).astype(jnp.bfloat16)
    grad_patch_unit = jnp.dot(mask_grad, class_low, preferred_element_type=jnp.float32) * mask_scale
    class_part = (
        jnp.einsum("rc,rd->cd", mask_grad, patch_low, preferred_element_type=jnp.float32)
        * mask_scale
    )
    class_total = lax.psum(class_part, ("grp", "seq"))
    grad_classes = class_back(class_total)[0].astype(jnp.bfloat16)
    class_proj_full = jnp.einsum(
        "cd,ce->de", class_emb, grad_classes, preferred_element_type=jnp.float32
    )
    class_emb_full = jnp.einsum(
        "ce,de->cd", grad_classes, proj_class, preferred_element_type=jnp.float32
    )
    grad_patches = patch_back(grad_patch_unit)[0].astype(jnp.bfloat16)
    grad_proj_patch = jnp.einsum(
        "rd,re->de", final_low, grad_patches, preferred_element_type=jnp.float32
    )
    grad_final = jnp.einsum(
        "re,de->rd", grad_patches, proj_patch, preferred_element_type=jnp.float32
    )
    grad_feed = grad_final.astype(jnp.bfloat16)
    grad_w_down = jnp.einsum("rf,rd->fd", active_low, grad_feed, preferred_element_type=jnp.float32)
    grad_bias_down = column_sum(grad_feed)
    grad_active = jnp.einsum("rd,fd->rf", grad_feed, w_down, preferred_element_type=jnp.float32)
    grad_hidden = gelu_back(grad_active)[0].astype(jnp.bfloat16)
    grad_w_up = jnp.einsum(
        "rd,rf->df", normed_two_low, grad_hidden, preferred_element_type=jnp.float32
    )
    grad_bias_up = column_sum(grad_hidden)
    grad_normed_two = jnp.einsum("rf,df->rd", grad_hidden, w_up, preferred_element_type=jnp.float32)
    grad_middle_norm, grad_ln2_gain, grad_ln2_bias = norm_two_back(grad_normed_two)
    grad_middle = grad_final + grad_middle_norm
    grad_branch = grad_middle.astype(jnp.bfloat16)
    grad_w_out = jnp.einsum(
        "rd,re->de", attended_low, grad_branch, preferred_element_type=jnp.float32
    )
    grad_bias_out = column_sum(grad_branch)
    grad_attended = jnp.einsum("re,de->rd", grad_branch, w_out, preferred_element_type=jnp.float32)
    grad_heads = grad_attended.astype(jnp.bfloat16).reshape(row_count, head_count, head_size)
    grad_query, grad_key_all, grad_value_all = attend_backward(
        query_heads,
        key_heads,
        value_heads,
        key_keep,
        grad_heads,
        log_mass,
        attended,
        score_scale,
        key_span,
    )
    grad_key_own, grad_value_own = (
        lax.psum_scatter(
            grad_key_all.astype(jnp.bfloat16), "seq", scatter_dimension=0, tiled=True
        ).astype(jnp.float32),
        lax.psum_scatter(
            grad_value_all.astype(jnp.bfloat16), "seq", scatter_dimension=0, tiled=True
        ).astype(jnp.float32),
    )
    grad_mixed = jnp.concatenate(
        [grad_query.reshape(row_count, model_width), grad_key_own, grad_value_own], axis=1
    ).astype(jnp.bfloat16)
    grad_w_qkv = jnp.einsum("rd,rm->dm", normed_low, grad_mixed, preferred_element_type=jnp.float32)
    grad_bias_all = column_sum(grad_mixed)
    grad_bias_query = grad_bias_all[:model_width]
    grad_bias_value = grad_bias_all[2 * model_width :]
    grad_normed_one = jnp.einsum("rm,dm->rd", grad_mixed, w_qkv, preferred_element_type=jnp.float32)
    grad_tokens_norm, grad_ln1_gain, grad_ln1_bias = norm_one_back(grad_normed_one)
    grad_tokens = (grad_middle + grad_tokens_norm).astype(jnp.bfloat16)
    row_parts = (
        lax.psum_scatter(grad_w_qkv, "grp", scatter_dimension=0, tiled=True),
        lax.psum_scatter(grad_w_out, "grp", scatter_dimension=0, tiled=True),
        lax.psum_scatter(grad_w_up, "grp", scatter_dimension=0, tiled=True),
        lax.psum_scatter(grad_w_down, "grp", scatter_dimension=0, tiled=True),
        lax.psum_scatter(grad_proj_patch, "grp", scatter_dimension=0, tiled=True),
        lax.psum_scatter(grad_ln1_gain, "grp", scatter_dimension=0, tiled=True),
        lax.psum_scatter(grad_ln1_bias, "grp", scatter_dimension=0, tiled=True),
        lax.psum_scatter(grad_bias_query, "grp", scatter_dimension=0, tiled=True),
        lax.psum_scatter(grad_bias_value, "grp", scatter_dimension=0, tiled=True),
        lax.psum_scatter(grad_bias_out, "grp", scatter_dimension=0, tiled=True),
        lax.psum_scatter(grad_ln2_gain, "grp", scatter_dimension=0, tiled=True),
        lax.psum_scatter(grad_ln2_bias, "grp", scatter_dimension=0, tiled=True),
        lax.psum_scatter(grad_bias_up, "grp", scatter_dimension=0, tiled=True),
        lax.psum_scatter(grad_bias_down, "grp", scatter_dimension=0, tiled=True),
    )
    matrix_parts = (
        lax.psum_scatter(
            row_parts[0].astype(jnp.bfloat16), "seq", scatter_dimension=1, tiled=True
        ).astype(jnp.float32),
        lax.psum_scatter(
            row_parts[1].astype(jnp.bfloat16), "seq", scatter_dimension=1, tiled=True
        ).astype(jnp.float32),
        lax.psum_scatter(
            row_parts[2].astype(jnp.bfloat16), "seq", scatter_dimension=1, tiled=True
        ).astype(jnp.float32),
        lax.psum_scatter(
            row_parts[3].astype(jnp.bfloat16), "seq", scatter_dimension=1, tiled=True
        ).astype(jnp.float32),
        lax.psum_scatter(
            row_parts[4].astype(jnp.bfloat16), "seq", scatter_dimension=1, tiled=True
        ).astype(jnp.float32),
    )
    vector_parts = lax.psum(
        (
            row_parts[5],
            row_parts[6],
            row_parts[7],
            row_parts[8],
            row_parts[9],
            row_parts[10],
            row_parts[11],
            row_parts[12],
            row_parts[13],
        ),
        "seq",
    )
    rows_each = model_width // grp_devices
    cols_each = model_width // seq_devices
    grp_here = lax.axis_index("grp")
    seq_here = lax.axis_index("seq")
    grad_proj_class = lax.dynamic_slice(
        class_proj_full, (grp_here * rows_each, seq_here * cols_each), (rows_each, cols_each)
    )
    grad_class_emb = lax.dynamic_slice_in_dim(class_emb_full, grp_here * rows_each, rows_each, 1)
    return (
        mask_out,
        grad_tokens,
        vector_parts[0],
        vector_parts[1],
        matrix_parts[0],
        vector_parts[2],
        vector_parts[3],
        matrix_parts[1],
        vector_parts[4],
        vector_parts[5],
        vector_parts[6],
        matrix_parts[2],
        vector_parts[7],
        matrix_parts[3],
        vector_parts[8],
        matrix_parts[4],
        grad_proj_class,
        grad_class_emb,
    )


def solution(mesh):
    return jax.shard_map(
        body,
        mesh=mesh,
        in_specs=(
            P(("grp", "seq"), None),
            P("grp"),
            P(),
            P(),
            P(),
            P(),
            P(),
            P(),
            P(),
            P(),
            P(),
            P(),
            P(),
            P(),
            P(),
            P(),
            P(),
            P(),
            P(("grp", "seq"), None),
        ),
        out_specs=(
            P(("grp", "seq"), None),
            P(("grp", "seq"), None),
            P("grp"),
            P("grp"),
            P("grp", "seq"),
            P("grp"),
            P("grp"),
            P("grp", "seq"),
            P("grp"),
            P("grp"),
            P("grp"),
            P("grp", "seq"),
            P("grp"),
            P("grp", "seq"),
            P("grp"),
            P("grp", "seq"),
            P("grp", "seq"),
            P(None, "grp"),
        ),
        check_vma=False,
    )
```

profile of v0, /device:TPU:0, one launch (start us, length us, event | category | flops | bytes accessed | tf_op | source)
XLA Modules:
  0.0 1562.4 jit_solution(7666178320111044407)
XLA Ops:
  30.2 29.2 %all-gather.5.cloned.1.call-done = bf16[3072,768]{1,0:T(8,128)(2,1)} async-done(((bf16[768,768]{1,0:T(8,128)(2,1)}), bf16[3072,768]{1,0:T(8,128)(2,1)}) %all-gather.5.cloned.1.call-update) | async-done | bytes 4718608 | tf_op jit(solution)/shard_map/all_gather | solution.py:183
  59.4 15.0 reshape.189
  74.4 13.5 copy.80
  88.0 165.2 %while.39 = (s32[]{:T(128)}, f32[12,768]{1,0:T(8,128)}, f32[12,768]{1,0:T(8,128)}, pred[6,512]{1,0:T(8,128)(4,1)S(1)}, bf16[6,512,12,64]{1,3,2,0:T(8,128)(2,1)},...) while((s32[]{:T(128)}, f32[12,768]{1,0:T(8,128)}, f32[12,768]{1,0:T(8,128)}, ...), condition=%wide.region_5.6_spmd.clone, body=%wide.region_2.5_spmd.clone.sunk | while | flops 637056000 | bytes 40196704 | solution.py:65
  88.0 12.4 bitcast_reduce_fusion.2
  115.5 12.3 bitcast_reduce_fusion.2
  143.0 12.3 bitcast_reduce_fusion.2
  170.6 12.3 bitcast_reduce_fusion.2
  198.1 12.3 bitcast_reduce_fusion.2
  211.9 10.8 fusion.145
  225.6 12.3 bitcast_reduce_fusion.2
  253.2 15.0 reshape.188
  268.1 13.6 copy.79
  283.2 61.1 %while.40 = (s32[]{:T(128)}, f32[768,12,64]{0,2,1:T(8,128)}, bf16[6,512,12,64]{1,3,2,0:T(8,128)(2,1)}, pred[6,512]{1,0:T(8,128)(4,1)S(1)}, bf16[6,512,12,64]{1,3...) while((s32[]{:T(128)}, f32[768,12,64]{0,2,1:T(8,128)}, ...), condition=%wide.region_7.8_spmd.clone, body=%wide.region_6.7_spmd.clone.sunk | while | flops 1228013568 | bytes 7522923 | solution.py:78
  350.3 28.6 %multiply_convert_fusion.1 = (bf16[768,3072]{1,0:T(8,128)(2,1)S(1)}, f32[768,3072]{1,0:T(8,128)}, f32[768,3072]{1,0:T(8,128)}) fusion(f32[3072]{0:T(1024)S(1)} %copy-done.54, bf16[768,3072]{1,0:T(8,128)(2,1)S(1)} %bitcast.171, f32[768,768]{0,1:T(8,128)S(1)} %get-tuple-element.449, f32[768]{0:T(1024)S(1)} %copy-done.57, f32[768]{0:T(1024)S(1)} %copy-done.42, ...), kind=kOutput, calls=%fused_computation.51 | convolution fusion | flops 3782541312 | bytes 30695424 | tf_op jit(solution)/shard_map/dot_general | solution.py:196
  395.1 13.0 convert_reduce_fusion
  433.9 291.4 %while.41 = (s32[]{:T(128)}, f32[768,12,64]{0,2,1:T(8,128)}, bf16[6,512,12,64]{1,3,2,0:T(8,128)(2,1)}, bf16[6,512,12,64]{1,3,2,0:T(8,128)(2,1)}, bf16[6,512,12,6...) while((s32[]{:T(128)}, f32[768,12,64]{0,2,1:T(8,128)}, ...), condition=%wide.region_16.17_spmd.clone, body=%wide.region_15.16_spmd.clone.sunk | while | flops 3068657664 | bytes 142766832 | solution.py:122
  445.0 10.9 multiply_convert_fusion.13
  470.6 11.9 bitcast_dynamic-update-slice_fusion.5
  493.2 10.8 multiply_convert_fusion.13
  519.2 11.9 bitcast_dynamic-update-slice_fusion.5
  567.8 11.9 bitcast_dynamic-update-slice_fusion.5
  616.3 11.9 bitcast_dynamic-update-slice_fusion.5
  664.8 11.9 bitcast_dynamic-update-slice_fusion.5
  713.3 11.8 bitcast_dynamic-update-slice_fusion.5
  784.4 50.4 %reduce-scatter.23.cloned.1.call-done = bf16[768,768]{0,1:T(8,128)(2,1)} async-done(((bf16[3072,768]{0,1:T(8,128)(2,1)}), bf16[768,768]{0,1:T(8,128)(2,1)}) %reduce-scatter.23.cloned.1.call-update) | async-done | bytes 1179664 | tf_op jit(solution)/shard_map/reduce_scatter | solution.py:264
  848.8 118.0 %all-reduce.13.cloned.1.call-done = f32[150,768]{1,0:T(8,128)} async-done(((f32[150,768]{1,0:T(8,128)}), f32[150,768]{1,0:T(8,128)}) %all-reduce.13.cloned.1.call-update) | async-done | bytes 460816 | tf_op jit(solution)/shard_map/psum | solution.py:215
  968.6 165.9 %reduce-scatter.33.cloned.1.call-done = f32[384,768]{1,0:T(8,128)} async-done(((f32[3072,768]{1,0:T(8,128)}), f32[384,768]{1,0:T(8,128)}) %reduce-scatter.33.cloned.1.call-update) | async-done | bytes 1179664 | tf_op jit(solution)/shard_map/reduce_scatter | solution.py:282
  1159.6 19.8 %reduce-scatter.39.cloned.1.call-done = bf16[192,96]{1,0:T(8,128)(2,1)} async-done(((bf16[768,96]{1,0:T(8,128)(2,1)}), bf16[192,96]{1,0:T(8,128)(2,1)}) %reduce-scatter.39.cloned.1.call-update) | async-done | bytes 36880
  1182.3 164.4 %reduce-scatter.29.cloned.1.call-done = f32[96,3072]{1,0:T(8,128)} async-done(((f32[768,3072]{1,0:T(8,128)}), f32[96,3072]{1,0:T(8,128)}) %reduce-scatter.29.cloned.1.call-update) | async-done | bytes 1179664 | tf_op jit(solution)/shard_map/reduce_scatter | solution.py:281
  1366.1 112.8 %reduce-scatter.25.cloned.1.call-done = f32[96,2304]{1,0:T(8,128)} async-done(((f32[768,2304]{1,0:T(8,128)}), f32[96,2304]{1,0:T(8,128)}) %reduce-scatter.25.cloned.1.call-update) | async-done | bytes 884752 | tf_op jit(solution)/shard_map/reduce_scatter | solution.py:279
  1484.3 36.8 %all-reduce.9 = (f32[768]{0:T(1024)}, f32[768]{0:T(1024)}, f32[768]{0:T(1024)}, f32[768]{0:T(1024)}, f32[768]{0:T(1024)}, /*index=5*/f32[768]{0:T(1024)}, f32[768]{0:T(1024)}, f32[3072]{0:T(1024)}, f32[768]{0:T(1024)}) all-reduce(f32[768]{0:T(1024)} %get-tuple-element.362, ...), channel_id=4, replica_groups=mesh['grp'=8,'seq'=4] {'grp'}, use_global_device_ids=true, to_apply=%region_22.23.clone | all-reduce | flops 9216 | bytes 73728
  (381 shorter events, 570.3 us)
Async XLA Ops:
  7.2 52.1 %all-gather.5.cloned.1.call-start = ((), (), s32[]{:S(2)}) async-start(), calls=%async_computation.13 | async-start | bytes 5898240 | tf_op jit(solution)/shard_map/all_gather | solution.py:183
  19.1 234.1 %all-gather.3.cloned.1.call-start = ((), (), s32[]{:S(2)}) async-start(), calls=%async_computation.12 | async-start | bytes 5898240 | tf_op jit(solution)/shard_map/all_gather | solution.py:184
  19.8 742.3 %reduce-scatter.35.cloned.1.call-start = ((), (), s32[]{:S(2)}) async-start(), calls=%async_computation.21 | async-start | bytes 2654208 | tf_op jit(solution)/shard_map/reduce_scatter | solution.py:283
  26.3 48.1 %copy-start.40 = (f32[150]{0:T(256)}, f32[150]{0:T(256)S(1)}, u32[]{:S(2)}) copy-start(f32[150]{0:T(256)S(1)} %add_rsqrt_fusion.1) | copy-start | bytes 1804
  346.6 32.3 %slice-start = ((s8[4718592]{0:T(1024)(128)(4,1)}), s8[4194304]{0:T(1024)(128)(4,1)S(1)}, s32[]{:S(2)}) async-start(s8[4718592]{0:T(1024)(128)(4,1)} %bitcast.168), calls=%async_computation.27 | async-start | bytes 8388608
  347.9 31.0 %copy-start.7 = (f32[768,768]{0,1:T(8,128)}, f32[768,768]{0,1:T(8,128)S(1)}, u32[]{:S(2)}) copy-start(f32[768,768]{0,1:T(8,128)S(1)} %get-tuple-element.449) | copy-start | bytes 7077892
  348.0 77.0 %copy-start.24 = (f32[768]{0:T(1024)}, f32[768]{0:T(1024)S(1)}, u32[]{:S(2)}) copy-start(f32[768]{0:T(1024)S(1)} %broadcast_multiply_fusion.1) | copy-start | bytes 9220
  350.3 74.7 %copy-start.38 = (f32[768]{0:T(1024)}, f32[768]{0:T(1024)S(1)}, u32[]{:S(2)}) copy-start(f32[768]{0:T(1024)S(1)} %fusion.66) | copy-start | bytes 9220
  350.3 28.7 %slice-start.1 = ((s8[4718592]{0:T(1024)(128)(4,1)}), s8[524288]{0:T(1024)(128)(4,1)S(1)}, s32[]{:S(2)}) async-start(s8[4718592]{0:T(1024)(128)(4,1)} %bitcast.168), calls=%async_computation.28 | async-start | bytes 1048576
  350.3 28.7 %copy-start.56 = (f32[768]{0:T(1024)S(1)}, f32[768]{0:T(1024)}, u32[]{:S(2)}) copy-start(f32[768]{0:T(1024)} %param.39) | copy-start | bytes 9220
  391.7 373.9 %reduce-scatter.27.cloned.1.call-start = ((), (), s32[]{:S(2)}) async-start(), calls=%async_computation.17 | async-start | bytes 2654208 | tf_op jit(solution)/shard_map/reduce_scatter | solution.py:280
  433.8 350.6 %reduce-scatter.21.cloned.1.call-start = ((), (), s32[]{:S(2)}) async-start(), calls=%async_computation.14 | async-start | bytes 5898240 | tf_op jit(solution)/shard_map/reduce_scatter | solution.py:261
  445.0 14.6 copy-start.2
  493.2 14.5 copy-start.2
  541.8 14.4 copy-start.2
  590.4 14.4 copy-start.2
  638.8 14.4 copy-start.2
  687.3 14.4 copy-start.2
  736.2 98.6 %reduce-scatter.23.cloned.1.call-start = ((), (), s32[]{:S(2)}) async-start(), calls=%async_computation.15 | async-start | bytes 5898240 | tf_op jit(solution)/shard_map/reduce_scatter | solution.py:264
  747.4 219.4 %all-reduce.13.cloned.1.call-start = ((), (), s32[]{:S(2)}) async-start(), calls=%async_computation.22 | async-start | bytes 933888 | tf_op jit(solution)/shard_map/psum | solution.py:215
  751.3 383.3 %reduce-scatter.33.cloned.1.call-start = ((), (), s32[]{:S(2)}) async-start(), calls=%async_computation.20 | async-start | bytes 10616832 | tf_op jit(solution)/shard_map/reduce_scatter | solution.py:282
  762.0 394.6 %reduce-scatter.43.cloned.1.call-start = ((), (), s32[]{:S(2)}) async-start(), calls=%async_computation.26 | async-start | bytes 245760
  765.5 413.9 %reduce-scatter.39.cloned.1.call-start = ((), (), s32[]{:S(2)}) async-start(), calls=%async_computation.24 | async-start | bytes 245760
  769.0 577.8 %reduce-scatter.29.cloned.1.call-start = ((), (), s32[]{:S(2)}) async-start(), calls=%async_computation.18 | async-start | bytes 10616832 | tf_op jit(solution)/shard_map/reduce_scatter | solution.py:281
  780.0 54.9 %copy-start.23 = (f32[768]{0:T(1024)S(1)}, f32[768]{0:T(1024)}, u32[]{:S(2)}) copy-start(f32[768]{0:T(1024)} %copy-done.22) | copy-start | bytes 9220
  780.0 54.9 %copy-start.32 = (f32[768]{0:T(1024)S(1)}, f32[768]{0:T(1024)}, u32[]{:S(2)}) copy-start(f32[768]{0:T(1024)} %copy-done.31) | copy-start | bytes 9220
  780.0 54.9 %copy-start.36 = (f32[768]{0:T(1024)S(1)}, f32[768]{0:T(1024)}, u32[]{:S(2)}) copy-start(f32[768]{0:T(1024)} %param.27) | copy-start | bytes 9220
  780.0 698.9 %reduce-scatter.25.cloned.1.call-start = ((), (), s32[]{:S(2)}) async-start(), calls=%async_computation.16 | async-start | bytes 7962624 | tf_op jit(solution)/shard_map/reduce_scatter | solution.py:279
  843.3 703.7 %reduce-scatter.41.cloned.1.call-start = ((), (), s32[]{:S(2)}) async-start(), calls=%async_computation.25 | async-start | bytes 737280
  848.8 290.8 %copy-start.41 = (f32[150]{0:T(256)S(1)}, f32[150]{0:T(256)}, u32[]{:S(2)}) copy-start(f32[150]{0:T(256)} %copy-done.40) | copy-start | bytes 1804
  1138.9 411.6 %reduce-scatter.31.cloned.1.call-start = ((), (), s32[]{:S(2)}) async-start(), calls=%async_computation.19 | async-start | bytes 737280 | tf_op jit(solution)/shard_map/reduce_scatter | solution.py:301
  1348.9 203.2 %reduce-scatter.37.cloned.1.call-start = ((), (), s32[]{:S(2)}) async-start(), calls=%async_computation.23 | async-start | bytes 737280
  (68 other events, 315.5 us)
Sparse Core Ops, SparseCore 0:
  19.2 40.1 all-gather.4
  60.9 37.4 all-gather.2
  391.8 69.1 reduce-scatter.34
  464.4 68.0 reduce-scatter.26
  736.4 48.0 reduce-scatter.20
  787.0 47.8 reduce-scatter.22
  840.2 126.5 all-reduce.12
  970.8 163.7 reduce-scatter.32
  1137.7 18.8 reduce-scatter.42
  1159.6 19.7 reduce-scatter.38
  1183.4 163.2 reduce-scatter.28
  1350.7 128.1 reduce-scatter.24
  1481.4 21.1 reduce-scatter.40
  1504.9 22.0 reduce-scatter.30
  1529.4 22.0 reduce-scatter.36
where the time goes:
time: 1570 us; the launch traced here: 1560 us
  waiting for transfers between devices  671 us (43%)
  matrix products  526 us (34%)
  local copies, waits for them, and re-layouts  171 us (11%)
  other arithmetic  131 us (8%)
  blocking collectives  43.3 us (3%)
  between operations  17.1 us (1%)
    reduce_scatter x1, waiting for transfers between devices, body(): lax.psum_scatter(grad_w_down, 'grp', scatter_dimension=0, tiled=True)  166 us
    reduce_scatter x1, waiting for transfers between devices, body(): lax.psum_scatter(grad_w_up, 'grp', scatter_dimension=0, tiled=True)  164 us
    dot_general x12, matrix products, score_block(): jnp.einsum('qhd,khd->hqk', query_heads, key_block, preferred_element_type...  138 us
    psum x1, waiting for transfers between devices, body(): class_total = lax.psum(class_part, ('grp', 'seq'))  118 us
    reduce_scatter x1, waiting for transfers between devices, body(): lax.psum_scatter(grad_w_qkv, 'grp', scatter_dimension=0, tiled=True)  113 us
    unnamed x148, local copies, waits for them, and re-layouts  81.5 us
    dot_general x6, matrix products, spread_grads(): jnp.einsum('hqk,qhd->khd', prob_rows.astype(jnp.bfloat16), grad_heads, pr...  71.3 us
    reduce_sum x6, other arithmetic, gather_stats(): jnp.sum(jnp.exp(scores - new_top[..., None]), axis=-1)  64.9 us
  transfers between devices with their start and end apart: 15, of which 9 were waited for; matrix products, arithmetic and copies ran while one was open for 41% of the time, Pallas kernels for 0%

commit v1 on v0

--- a/solution.py
+++ b/solution.py
@@ -154,6 +154,14 @@
     class_emb,
     d_masks,
 ):
+
+    def run_lane_in(u_in):
+        ax_name = "grp"
+        mesh_ax = "seq"
+        for ix in (mesh_ax, ax_name):
+            u_in = lax.psum(u_in, axis_name=ix)
+        return u_in
+
     row_count, model_width = tokens_in.shape
     head_size = HEAD_DIM
     head_count = model_width // head_size
@@ -212,7 +220,7 @@
         jnp.einsum("rc,rd->cd", mask_grad, patch_low, preferred_element_type=jnp.float32)
         * mask_scale
     )
-    class_total = lax.psum(class_part, ("grp", "seq"))
+    class_total = run_lane_in(class_part)
     grad_classes = class_back(class_total)[0].astype(jnp.bfloat16)
     class_proj_full = jnp.einsum(
         "cd,ce->de", class_emb, grad_classes, preferred_element_type=jnp.float32

time: 1570 us -> 1520 us (0.968)
  waiting for transfers between devices: 671 us -> 616 us
    psum x1 -> x2, waiting for transfers between devices: 118 us -> 61.8 us  [run_lane_in(): u_in = lax.psum(u_in, axis_name=ix)]
    unnamed x148 -> x162, local copies, waits for them, and re-layouts: 81.5 us -> 82 us
  transfers between devices with their start and end apart: 15 -> 16, of which waited for: 9 -> 9; matrix products, arithmetic and copies ran while one was open for 41% -> 43% of each run, Pallas kernels for 0% -> 0%
where the time goes in v1:
time: 1520 us; the launch traced here: 1510 us
  waiting for transfers between devices  616 us (41%)
  matrix products  527 us (35%)
  local copies, waits for them, and re-layouts  171 us (11%)
  other arithmetic  134 us (9%)
  blocking collectives  43.3 us (3%)
  between operations  17.2 us (1%)
    reduce_scatter x1, waiting for transfers between devices, body(): lax.psum_scatter(grad_w_down, 'grp', scatter_dimension=0, tiled=True)  164 us
    reduce_scatter x1, waiting for transfers between devices, body(): lax.psum_scatter(grad_w_up, 'grp', scatter_dimension=0, tiled=True)  164 us
    dot_general x12, matrix products, score_block(): jnp.einsum('qhd,khd->hqk', query_heads, key_block, preferred_element_type...  138 us
    reduce_scatter x1, waiting for transfers between devices, body(): lax.psum_scatter(grad_w_qkv, 'grp', scatter_dimension=0, tiled=True)  113 us
    unnamed x162, local copies, waits for them, and re-layouts  82 us
    dot_general x6, matrix products, spread_grads(): jnp.einsum('hqk,qhd->khd', prob_rows.astype(jnp.bfloat16), grad_heads, pr...  71.6 us
    reduce_sum x6, other arithmetic, gather_stats(): jnp.sum(jnp.exp(scores - new_top[..., None]), axis=-1)  64.9 us
    dot_general x6, matrix products, spread_grads(): jnp.einsum('qhd,khd->hqk', grad_heads, value_block, preferred_element_typ...  64.5 us
  transfers between devices with their start and end apart: 16, of which 9 were waited for; matrix products, arithmetic and copies ran while one was open for 43% of the time, Pallas kernels for 0%

profile of v1, /device:TPU:0, one launch (start us, length us, event | category | flops | bytes accessed | tf_op | source)
XLA Modules:
  0.0 1511.1 jit_solution(10854293935117365652)
XLA Ops:
  30.2 29.2 %all-gather.5.cloned.1.call-done = bf16[3072,768]{1,0:T(8,128)(2,1)} async-done(((bf16[768,768]{1,0:T(8,128)(2,1)}), bf16[3072,768]{1,0:T(8,128)(2,1)}) %all-gather.5.cloned.1.call-update) | async-done | bytes 4718608 | tf_op jit(solution)/shard_map/all_gather | solution.py:191
  59.4 15.0 reshape.189
  74.4 13.5 copy.80
  88.0 165.3 %while.39 = (s32[]{:T(128)}, f32[12,768]{1,0:T(8,128)}, f32[12,768]{1,0:T(8,128)}, pred[6,512]{1,0:T(8,128)(4,1)S(1)}, bf16[6,512,12,64]{1,3,2,0:T(8,128)(2,1)},...) while((s32[]{:T(128)}, f32[12,768]{1,0:T(8,128)}, f32[12,768]{1,0:T(8,128)}, ...), condition=%wide.region_5.6_spmd.clone, body=%wide.region_2.5_spmd.clone.sunk | while | flops 637056000 | bytes 40196704 | solution.py:65
  88.0 12.4 bitcast_reduce_fusion.2
  101.8 10.8 fusion.145
  115.5 12.3 bitcast_reduce_fusion.2
  143.1 12.3 bitcast_reduce_fusion.2
  170.6 12.3 bitcast_reduce_fusion.2
  198.2 12.3 bitcast_reduce_fusion.2
  225.8 12.3 bitcast_reduce_fusion.2
  253.3 15.0 reshape.188
  268.3 13.6 copy.79
  283.3 61.1 %while.40 = (s32[]{:T(128)}, f32[768,12,64]{0,2,1:T(8,128)}, bf16[6,512,12,64]{1,3,2,0:T(8,128)(2,1)}, pred[6,512]{1,0:T(8,128)(4,1)S(1)}, bf16[6,512,12,64]{1,3...) while((s32[]{:T(128)}, f32[768,12,64]{0,2,1:T(8,128)}, ...), condition=%wide.region_7.8_spmd.clone, body=%wide.region_6.7_spmd.clone.sunk | while | flops 1228013568 | bytes 7522923 | solution.py:78
  350.5 28.6 %multiply_convert_fusion.1 = (bf16[768,3072]{1,0:T(8,128)(2,1)S(1)}, f32[768,3072]{1,0:T(8,128)}, f32[768,3072]{1,0:T(8,128)}) fusion(f32[3072]{0:T(1024)S(1)} %copy-done.58, bf16[768,3072]{1,0:T(8,128)(2,1)S(1)} %bitcast.171, f32[768,768]{0,1:T(8,128)S(1)} %get-tuple-element.449, f32[768]{0:T(1024)S(1)} %copy-done.61, f32[768]{0:T(1024)S(1)} %copy-done.45, ...), kind=kOutput, calls=%fused_computation.51 | convolution fusion | flops 3782541312 | bytes 30695424 | tf_op jit(solution)/shard_map/dot_general | solution.py:204
  401.0 13.0 convert_reduce_fusion
  440.2 292.5 %while.41 = (s32[]{:T(128)}, f32[768,12,64]{0,2,1:T(8,128)}, bf16[6,512,12,64]{1,3,2,0:T(8,128)(2,1)}, bf16[6,512,12,64]{1,3,2,0:T(8,128)(2,1)}, bf16[6,512,12,6...) while((s32[]{:T(128)}, f32[768,12,64]{0,2,1:T(8,128)}, ...), condition=%wide.region_16.17_spmd.clone, body=%wide.region_15.16_spmd.clone.sunk | while | flops 3068657664 | bytes 142766832 | solution.py:122
  476.9 12.1 bitcast_dynamic-update-slice_fusion.5
  499.7 10.8 multiply_convert_fusion.13
  525.9 12.1 bitcast_dynamic-update-slice_fusion.5
  548.7 10.9 multiply_convert_fusion.13
  574.9 11.9 bitcast_dynamic-update-slice_fusion.5
  623.4 11.9 bitcast_dynamic-update-slice_fusion.5
  672.1 11.9 bitcast_dynamic-update-slice_fusion.5
  720.7 11.9 bitcast_dynamic-update-slice_fusion.5
  791.6 50.4 %reduce-scatter.23.cloned.1.call-done = bf16[768,768]{0,1:T(8,128)(2,1)} async-done(((bf16[3072,768]{0,1:T(8,128)(2,1)}), bf16[768,768]{0,1:T(8,128)(2,1)}) %reduce-scatter.23.cloned.1.call-update) | async-done | bytes 1179664 | tf_op jit(solution)/shard_map/reduce_scatter | solution.py:272
  856.0 61.8 %all-reduce.16.cloned.1.call-done = f32[150,768]{1,0:T(8,128)} async-done(((f32[150,768]{1,0:T(8,128)}), f32[150,768]{1,0:T(8,128)}) %all-reduce.16.cloned.1.call-update) | async-done | bytes 460816 | tf_op jit(solution)/shard_map/psum | solution.py:162
  919.7 164.5 %reduce-scatter.33.cloned.1.call-done = f32[384,768]{1,0:T(8,128)} async-done(((f32[3072,768]{1,0:T(8,128)}), f32[384,768]{1,0:T(8,128)}) %reduce-scatter.33.cloned.1.call-update) | async-done | bytes 1179664 | tf_op jit(solution)/shard_map/reduce_scatter | solution.py:290
  1108.8 19.8 %reduce-scatter.39.cloned.1.call-done = bf16[192,96]{1,0:T(8,128)(2,1)} async-done(((bf16[768,96]{1,0:T(8,128)(2,1)}), bf16[192,96]{1,0:T(8,128)(2,1)}) %reduce-scatter.39.cloned.1.call-update) | async-done | bytes 36880
  1131.6 164.0 %reduce-scatter.29.cloned.1.call-done = f32[96,3072]{1,0:T(8,128)} async-done(((f32[768,3072]{1,0:T(8,128)}), f32[96,3072]{1,0:T(8,128)}) %reduce-scatter.29.cloned.1.call-update) | async-done | bytes 1179664 | tf_op jit(solution)/shard_map/reduce_scatter | solution.py:289
  1314.8 112.7 %reduce-scatter.25.cloned.1.call-done = f32[96,2304]{1,0:T(8,128)} async-done(((f32[768,2304]{1,0:T(8,128)}), f32[96,2304]{1,0:T(8,128)}) %reduce-scatter.25.cloned.1.call-update) | async-done | bytes 884752 | tf_op jit(solution)/shard_map/reduce_scatter | solution.py:287
  1432.9 36.8 %all-reduce.9 = (f32[768]{0:T(1024)}, f32[768]{0:T(1024)}, f32[768]{0:T(1024)}, f32[768]{0:T(1024)}, f32[768]{0:T(1024)}, /*index=5*/f32[768]{0:T(1024)}, f32[768]{0:T(1024)}, f32[3072]{0:T(1024)}, f32[768]{0:T(1024)}) all-reduce(f32[768]{0:T(1024)} %get-tuple-element.362, ...), channel_id=4, replica_groups=mesh['grp'=8,'seq'=4] {'grp'}, use_global_device_ids=true, to_apply=%region_22.23.clone | all-reduce | flops 9216 | bytes 73728
  (398 shorter events, 576.5 us)
Async XLA Ops:
  7.2 52.2 %all-gather.5.cloned.1.call-start = ((), (), s32[]{:S(2)}) async-start(), calls=%async_computation.13 | async-start | bytes 5898240 | tf_op jit(solution)/shard_map/all_gather | solution.py:191
  19.1 234.2 %all-gather.3.cloned.1.call-start = ((), (), s32[]{:S(2)}) async-start(), calls=%async_computation.12 | async-start | bytes 5898240 | tf_op jit(solution)/shard_map/all_gather | solution.py:192
  19.8 735.1 %all-reduce.14.cloned.1.call-start = ((), (), s32[]{:S(2)}) async-start(), calls=%async_computation.22 | async-start | bytes 933888 | tf_op jit(solution)/shard_map/psum | solution.py:162
  26.3 48.2 %copy-start.43 = (f32[150]{0:T(256)}, f32[150]{0:T(256)S(1)}, u32[]{:S(2)}) copy-start(f32[150]{0:T(256)S(1)} %add_rsqrt_fusion.1) | copy-start | bytes 1804
  346.8 32.3 %slice-start = ((s8[4718592]{0:T(1024)(128)(4,1)}), s8[4194304]{0:T(1024)(128)(4,1)S(1)}, s32[]{:S(2)}) async-start(s8[4718592]{0:T(1024)(128)(4,1)} %bitcast.168), calls=%async_computation.28 | async-start | bytes 8388608
  348.1 31.0 %copy-start.7 = (f32[768,768]{0,1:T(8,128)}, f32[768,768]{0,1:T(8,128)S(1)}, u32[]{:S(2)}) copy-start(f32[768,768]{0,1:T(8,128)S(1)} %get-tuple-element.449) | copy-start | bytes 7077892
  348.1 82.7 %copy-start.26 = (f32[768]{0:T(1024)}, f32[768]{0:T(1024)S(1)}, u32[]{:S(2)}) copy-start(f32[768]{0:T(1024)S(1)} %broadcast_multiply_fusion.1) | copy-start | bytes 9220
  350.4 80.4 %copy-start.41 = (f32[768]{0:T(1024)}, f32[768]{0:T(1024)S(1)}, u32[]{:S(2)}) copy-start(f32[768]{0:T(1024)S(1)} %fusion.66) | copy-start | bytes 9220
  350.5 28.7 %slice-start.1 = ((s8[4718592]{0:T(1024)(128)(4,1)}), s8[524288]{0:T(1024)(128)(4,1)S(1)}, s32[]{:S(2)}) async-start(s8[4718592]{0:T(1024)(128)(4,1)} %bitcast.168), calls=%async_computation.29 | async-start | bytes 1048576
  350.5 28.7 %copy-start.60 = (f32[768]{0:T(1024)S(1)}, f32[768]{0:T(1024)}, u32[]{:S(2)}) copy-start(f32[768]{0:T(1024)} %param.39) | copy-start | bytes 9220
  387.6 378.9 %reduce-scatter.35.cloned.1.call-start = ((), (), s32[]{:S(2)}) async-start(), calls=%async_computation.21 | async-start | bytes 2654208 | tf_op jit(solution)/shard_map/reduce_scatter | solution.py:291
  400.9 369.0 %reduce-scatter.27.cloned.1.call-start = ((), (), s32[]{:S(2)}) async-start(), calls=%async_computation.17 | async-start | bytes 2654208 | tf_op jit(solution)/shard_map/reduce_scatter | solution.py:288
  440.1 351.4 %reduce-scatter.21.cloned.1.call-start = ((), (), s32[]{:S(2)}) async-start(), calls=%async_computation.14 | async-start | bytes 5898240 | tf_op jit(solution)/shard_map/reduce_scatter | solution.py:269
  451.4 14.5 copy-start.2
  499.6 14.6 copy-start.2
  548.7 14.6 copy-start.2
  646.0 14.4 copy-start.2
  743.9 98.1 %reduce-scatter.23.cloned.1.call-start = ((), (), s32[]{:S(2)}) async-start(), calls=%async_computation.15 | async-start | bytes 5898240 | tf_op jit(solution)/shard_map/reduce_scatter | solution.py:272
  754.9 162.9 %all-reduce.16.cloned.1.call-start = ((), (), s32[]{:S(2)}) async-start(), calls=%async_computation.23 | async-start | bytes 933888 | tf_op jit(solution)/shard_map/psum | solution.py:162
  755.6 328.5 %reduce-scatter.33.cloned.1.call-start = ((), (), s32[]{:S(2)}) async-start(), calls=%async_computation.20 | async-start | bytes 10616832 | tf_op jit(solution)/shard_map/reduce_scatter | solution.py:290
  766.4 339.5 %reduce-scatter.43.cloned.1.call-start = ((), (), s32[]{:S(2)}) async-start(), calls=%async_computation.27 | async-start | bytes 245760
  769.9 358.8 %reduce-scatter.39.cloned.1.call-start = ((), (), s32[]{:S(2)}) async-start(), calls=%async_computation.25 | async-start | bytes 245760
  773.3 522.3 %reduce-scatter.29.cloned.1.call-start = ((), (), s32[]{:S(2)}) async-start(), calls=%async_computation.18 | async-start | bytes 10616832 | tf_op jit(solution)/shard_map/reduce_scatter | solution.py:289
  784.3 57.7 %copy-start.25 = (f32[768]{0:T(1024)S(1)}, f32[768]{0:T(1024)}, u32[]{:S(2)}) copy-start(f32[768]{0:T(1024)} %copy-done.24) | copy-start | bytes 9220
  784.3 57.7 %copy-start.35 = (f32[768]{0:T(1024)S(1)}, f32[768]{0:T(1024)}, u32[]{:S(2)}) copy-start(f32[768]{0:T(1024)} %copy-done.34) | copy-start | bytes 9220
  784.3 57.7 %copy-start.39 = (f32[768]{0:T(1024)S(1)}, f32[768]{0:T(1024)}, u32[]{:S(2)}) copy-start(f32[768]{0:T(1024)} %param.27) | copy-start | bytes 9220
  784.3 57.7 %copy-start.64 = (f32[768]{0:T(1024)S(1)}, f32[768]{0:T(1024)}, u32[]{:S(2)}) copy-start(f32[768]{0:T(1024)} %param.28) | copy-start | bytes 9220
  784.3 643.1 %reduce-scatter.25.cloned.1.call-start = ((), (), s32[]{:S(2)}) async-start(), calls=%async_computation.16 | async-start | bytes 7962624 | tf_op jit(solution)/shard_map/reduce_scatter | solution.py:287
  850.4 645.3 %reduce-scatter.41.cloned.1.call-start = ((), (), s32[]{:S(2)}) async-start(), calls=%async_computation.26 | async-start | bytes 737280
  856.0 233.2 %copy-start.44 = (f32[150]{0:T(256)S(1)}, f32[150]{0:T(256)}, u32[]{:S(2)}) copy-start(f32[150]{0:T(256)} %copy-done.43) | copy-start | bytes 1804
  1088.4 410.8 %reduce-scatter.31.cloned.1.call-start = ((), (), s32[]{:S(2)}) async-start(), calls=%async_computation.19 | async-start | bytes 737280 | tf_op jit(solution)/shard_map/reduce_scatter | solution.py:309
  1297.8 203.0 %reduce-scatter.37.cloned.1.call-start = ((), (), s32[]{:S(2)}) async-start(), calls=%async_computation.24 | async-start | bytes 737280
  (76 other events, 368.2 us)
Sparse Core Ops, SparseCore 0:
  19.2 40.1 all-gather.4
  61.0 37.4 all-gather.2
  387.7 32.5 all-reduce.13
  424.1 69.3 reduce-scatter.34
  497.3 68.0 reduce-scatter.26
  744.0 47.5 reduce-scatter.20
  794.1 47.8 reduce-scatter.22
  845.8 71.9 all-reduce.15
  921.4 162.6 reduce-scatter.32
  1087.0 18.8 reduce-scatter.42
  1108.9 19.7 reduce-scatter.38
  1132.1 163.4 reduce-scatter.28
  1299.3 128.1 reduce-scatter.24
  1430.0 21.0 reduce-scatter.40
  1453.6 22.0 reduce-scatter.30
  1478.2 22.0 reduce-scatter.36
